TPU v7x, 256 devices: a whole 4x4x8 slice. The times are simulated.
256 devices in a mesh: section: 16 (over x_lo, y, core), expert: 16 (over z, x_hi).
Axes of the slice: x: 4 (x_hi: 2, x_lo: 2; x = x_hi * 2 + x_lo), y: 4, z: 8, core: 2. Of those that a mesh axis runs over, the one named last changes fastest.
Arguments:
- activations: bfloat16 [16, 2048, 4096], P('section', 'expert'), may hold values from -6 to 6
- norm_gain: bfloat16 [16, 4096], P('section'), may hold values from 0.099609375 to 1.8984375
- w_gate: bfloat16 [16, 4096, 6144], P('section', None, 'expert'), may hold values from -0.09375 to 0.09375
- w_up: bfloat16 [16, 4096, 6144], P('section', None, 'expert'), may hold values from -0.09375 to 0.09375
- w_down: bfloat16 [16, 6144, 4096], P('section', 'expert'), may hold values from -0.15625 to 0.15625
- expert_ids: int32 [2, 16, 2048, 8], P(None, 'section', 'expert'), may hold values from 0 to 127, as said below
- route_weights: float32 [2, 16, 2048, 8], P(None, 'section', 'expert'), may hold values from 0.5 to 2
Outputs:
- final_state: bfloat16 [16, 2048, 4096], P('section', 'expert')
Inputs may be any that keep to these rules, and one draw needn't show every extreme that they name: `expert_ids`: each token names 8 different experts. In every aligned block of 128 tokens (one device's tokens), at every stop and section, each expert below 4 is named by at most 16 tokens, and at every stop and section one of them is named by exactly 16 tokens in every block.
All inputs are finite; a program needn't handle non-finite values.
Results may differ from a plain program's by a relative error of at most 0.007.
Values may be sent and summed in bfloat16 or wider, within the bound.
A program may use at most 64 MiB of HBM per device.

v0:
```python
import jax
import jax.numpy as jnp
from jax import lax
from jax.sharding import PartitionSpec as P

SPECIALIST_SPAN = 4


def passed_along(value, axis, steps):
    count = lax.axis_size(axis)
    pairs = [(source, (source + steps) % count) for source in range(count)]
    return lax.ppermute(value, axis, pairs)


def root_norm(values, norm_gain):
    as_float = values.astype(jnp.float32)
    scale_factor = lax.rsqrt(jnp.mean(as_float * as_float, axis=-1, keepdims=True) + 1e-06)
    return (as_float * scale_factor * norm_gain.astype(jnp.float32)).astype(jnp.bfloat16)


def one_stop(carried, norm_gain, w_gate, w_up, w_down, picked, weights):
    tokens = carried.shape[0]
    model_width = carried.shape[1]
    capacity = tokens // 8
    devices = lax.axis_size("expert")
    group_size = max(1, devices // SPECIALIST_SPAN)
    per_device = max(1, SPECIALIST_SPAN // devices)
    groups = devices // group_size
    normed = root_norm(carried, norm_gain)
    experts = jnp.arange(SPECIALIST_SPAN, dtype=jnp.int32)
    name_hits = picked[:, :, None] == experts
    matched = jnp.any(name_hits, axis=1)
    factor = jnp.sum(jnp.where(name_hits, weights[:, :, None], 0.0), axis=1)
    slot_rank = jnp.cumsum(matched.astype(jnp.int32), axis=0) - 1
    slot_ids = jnp.arange(capacity, dtype=jnp.int32)
    select = jnp.logical_and(
        matched.T[:, None, :], slot_rank.T[:, None, :] == slot_ids[None, :, None]
    )
    dispatch = jnp.einsum(
        "ect,td->ecd", select.astype(jnp.bfloat16), normed, preferred_element_type=jnp.float32
    ).astype(jnp.bfloat16)
    hid_per = w_gate.shape[1] // per_device
    gate_w = w_gate.reshape(model_width, per_device, hid_per)
    up_w = w_up.reshape(model_width, per_device, hid_per)
    down_w = w_down.reshape(per_device, hid_per, model_width)
    grouped = dispatch.reshape(groups, 1, per_device, capacity, model_width)
    outgoing = jnp.broadcast_to(grouped, (groups, group_size, per_device, capacity, model_width))
    outgoing = outgoing.reshape(devices, per_device, capacity, model_width)
    slot_rows = lax.all_to_all(outgoing, "expert", split_axis=0, concat_axis=0, tiled=True)
    gate_act = jnp.einsum("skmd,dkh->skmh", slot_rows, gate_w, preferred_element_type=jnp.float32)
    up_act = jnp.einsum("skmd,dkh->skmh", slot_rows, up_w, preferred_element_type=jnp.float32)
    hidden = (jax.nn.silu(gate_act) * up_act).astype(jnp.bfloat16)
    partials = lax.all_to_all(
        jnp.einsum("skmh,khd->skmd", hidden, down_w, preferred_element_type=jnp.float32),
        "expert",
        split_axis=0,
        concat_axis=0,
        tiled=True,
    )
    results = jnp.sum(
        partials.reshape(groups, group_size, per_device, capacity, model_width), axis=1
    )
    results = results.reshape(SPECIALIST_SPAN, capacity, model_width).astype(jnp.bfloat16)
    combine = jnp.where(select, factor.T[:, None, :], 0.0)
    mixture = jnp.einsum(
        "ect,ecd->td", combine, results.astype(jnp.float32), precision=lax.Precision.HIGHEST
    )
    return (carried.astype(jnp.float32) + mixture).astype(jnp.bfloat16)


def body(activations, norm_gain, w_gate, w_up, w_down, expert_ids, route_weights):
    carried = activations[0]
    stop_count = expert_ids.shape[0]
    for stop_index in range(stop_count):
        carried = one_stop(
            carried,
            norm_gain[0],
            w_gate[0],
            w_up[0],
            w_down[0],
            expert_ids[stop_index, 0],
            route_weights[stop_index, 0],
        )
        if stop_index + 1 < stop_count:
            carried = passed_along(carried, "section", 1)
    return carried[None]


def solution(mesh):
    return jax.shard_map(
        body,
        mesh=mesh,
        in_specs=(
            P("section", "expert", None),
            P("section", None),
            P("section", None, "expert"),
            P("section", None, "expert"),
            P("section", "expert", None),
            P(None, "section", "expert", None),
            P(None, "section", "expert", None),
        ),
        out_specs=P("section", "expert", None),
        check_vma=False,
    )
```

profile of v0, /device:TPU:24, one launch (start us, length us, event | category | flops | bytes accessed | tf_op | source)
XLA Modules:
  0.0 373.4 jit_solution(6043589702203790056)
XLA Ops:
  0.0 0.0 copy-start
  0.0 1.7 fusion.18
  1.7 0.7 slice_bitcast_fusion.1
  2.4 0.0 copy-start.7
  2.4 0.7 mul.69
  3.2 0.0 copy-start.4
  3.2 0.1 copy.26
  3.3 0.2 reduce_window_sum.17
  3.5 0.1 copy.27
  3.5 1.8 convolution_convert_fusion.1
  5.3 0.2 broadcast_in_dim.76
  5.5 0.0 copy-done.7
  5.5 0.0 copy-done.4
  5.6 0.0 copy-start.9
  5.6 63.5 %all_to_all.20 = bf16[16,1,16,4096]{3,2,1,0:T(8,128)(2,1)S(1)} all-to-all(bf16[16,1,16,4096]{3,2,1,0:T(8,128)(2,1)S(1)} %bitcast.197), channel_id=1, replica_groups=mesh['section'=16,'expert'=16] {'expert'}, dimensions={0} | all-to-all | bytes 4194304 | tf_op jit(solution)/shard_map/all_to_all | solution.py:49
  69.0 0.0 copy-start.1
  69.0 1.3 copy-done.1
  70.4 0.0 copy-done.9
  70.4 1.3 fusion.25
  71.7 0.0 copy-done
  71.7 6.9 %convolution_bitcast_fusion.1 = f32[16,1,16,4096]{3,2,1,0:T(8,128)} fusion(bf16[1,384,4096]{2,1,0:T(8,128)(2,1)S(1)} %copy-done, bf16[1,4096,384]{2,1,0:T(8,128)(2,1)} %param.10, bf16[16,1,16,4096]{3,2,1,0:T(8,128)(2,1)} %copy-done.1, f32[16,1,16,384]{3,2,0,1:T(8,128)S(1)} %fusion.25), kind=kOutput, calls=%fused_computation.1 | convolution fusion | flops 1611202560 | bytes 12976128 | tf_op jit(solution)/shard_map/skmh,khd->skmd/dot_general | solution.py:54
  78.6 4.7 %all-to-all-start.1 = ((f32[16,1,16,4096]{3,2,1,0:T(8,128)}), f32[16,1,16,4096]{3,2,1,0:T(8,128)}, u32[]{:S(2)}, u32[]{:S(2)}) async-start(f32[16,1,16,4096]{3,2,1,0:T(8,128)} %convolution_bitcast_fusion.1), calls=%async_computation.1 | async-start | bytes 8388608 | tf_op jit(solution)/shard_map/all_to_all | solution.py:53
  83.3 0.0 copy-done.6
  83.3 96.9 %all-to-all-done.1 = f32[16,1,16,4096]{3,2,1,0:T(8,128)} async-done(((f32[16,1,16,4096]{3,2,1,0:T(8,128)}), f32[16,1,16,4096]{3,2,1,0:T(8,128)}, u32[]{:S(2)}, u32[]{:S(2)}) %all-to-all-start.1) | async-done | bytes 4194336 | tf_op jit(solution)/shard_map/all_to_all | solution.py:53
  180.2 2.7 bitcast_reduce_fusion.1
  183.0 0.0 copy-start.5
  183.0 0.0 copy-done.3
  183.0 0.0 copy-done.8
  183.0 2.1 fusion.3
  185.1 0.0 collective-permute-start
  185.1 0.1 copy.29
  185.2 0.2 reduce_window_sum.18
  185.4 0.1 copy.30
  185.5 14.2 %collective-permute-done = bf16[128,4096]{1,0:T(8,128)(2,1)} collective-permute-done((bf16[128,4096]{1,0:T(8,128)(2,1)}, bf16[128,4096]{1,0:T(8,128)(2,1)}, u32[]{:S(2)}, u32[]{:S(2)}) %collective-permute-start) | collective-permute-done | bytes 1048608 | tf_op jit(solution)/shard_map/ppermute | solution.py:12
  199.6 1.5 fusion.15
  201.1 0.0 copy-done.5
  201.1 1.7 convolution_convert_fusion
  202.9 0.2 broadcast_in_dim.81
  203.1 0.0 copy-start.10
  203.2 55.1 %all_to_all.21 = bf16[16,1,16,4096]{3,2,1,0:T(8,128)(2,1)S(1)} all-to-all(bf16[16,1,16,4096]{3,2,1,0:T(8,128)(2,1)S(1)} %bitcast.198), channel_id=1, replica_groups=mesh['section'=16,'expert'=16] {'expert'}, dimensions={0} | all-to-all | bytes 4194304 | tf_op jit(solution)/shard_map/all_to_all | solution.py:49
  258.2 1.3 copy-done.2
  259.5 0.0 copy-done.10
  259.5 1.3 fusion.30
  260.9 6.9 %convolution_bitcast_fusion = f32[16,1,16,4096]{3,2,1,0:T(8,128)} fusion(bf16[1,384,4096]{2,1,0:T(8,128)(2,1)S(1)} %copy-done, bf16[1,4096,384]{2,1,0:T(8,128)(2,1)} %param.10, bf16[16,1,16,4096]{3,2,1,0:T(8,128)(2,1)} %copy-done.2, f32[16,1,16,384]{3,2,0,1:T(8,128)S(1)} %fusion.30), kind=kOutput, calls=%fused_computation | convolution fusion | flops 1611202560 | bytes 12976128 | tf_op jit(solution)/shard_map/skmh,khd->skmd/dot_general | solution.py:54
  267.7 4.5 %all-to-all-start.3 = ((f32[16,1,16,4096]{3,2,1,0:T(8,128)}), f32[16,1,16,4096]{3,2,1,0:T(8,128)}, u32[]{:S(2)}, u32[]{:S(2)}) async-start(f32[16,1,16,4096]{3,2,1,0:T(8,128)} %convolution_bitcast_fusion), calls=%async_computation.3 | async-start | bytes 8388608 | tf_op jit(solution)/shard_map/all_to_all | solution.py:53
  272.3 95.2 %all-to-all-done.3 = f32[16,1,16,4096]{3,2,1,0:T(8,128)} async-done(((f32[16,1,16,4096]{3,2,1,0:T(8,128)}), f32[16,1,16,4096]{3,2,1,0:T(8,128)}, u32[]{:S(2)}, u32[]{:S(2)}) %all-to-all-start.3) | async-done | bytes 4194336 | tf_op jit(solution)/shard_map/all_to_all | solution.py:53
  367.5 2.6 bitcast_reduce_fusion
  370.2 3.3 fusion.4
  (15 shorter events, 0.1 us)
Async XLA Ops:
  0.0 71.7 %copy-start = (bf16[1,384,4096]{2,1,0:T(8,128)(2,1)S(1)}, bf16[1,384,4096]{2,1,0:T(8,128)(2,1)}, u32[]{:S(2)}) copy-start(bf16[1,384,4096]{2,1,0:T(8,128)(2,1)} %param.11) | copy-start | bytes 9437188
  2.4 3.1 copy-start.7
  3.2 2.4 copy-start.4
  5.6 64.8 %copy-start.9 = (bf16[1,4096,384]{2,1,0:T(8,128)(2,1)S(1)}, bf16[1,4096,384]{2,1,0:T(8,128)(2,1)}, u32[]{:S(2)}) copy-start(bf16[1,4096,384]{2,1,0:T(8,128)(2,1)} %param.9) | copy-start | bytes 9437188
  69.0 1.3 copy-start.1
  78.6 4.7 %copy-start.6 = (f32[2,1,128,8]{2,3,1,0:T(8,128)S(1)}, f32[2,1,128,8]{2,3,1,0:T(8,128)}, u32[]{:S(2)}) copy-start(f32[2,1,128,8]{2,3,1,0:T(8,128)} %param.13) | copy-start | bytes 24580
  78.6 101.6 %all-to-all-start.1 = ((f32[16,1,16,4096]{3,2,1,0:T(8,128)}), f32[16,1,16,4096]{3,2,1,0:T(8,128)}, u32[]{:S(2)}, u32[]{:S(2)}) async-start(f32[16,1,16,4096]{3,2,1,0:T(8,128)} %convolution_bitcast_fusion.1), calls=%async_computation.1 | async-start | bytes 8388608 | tf_op jit(solution)/shard_map/all_to_all | solution.py:53
  180.2 2.7 copy-start.3
  180.2 2.7 copy-start.8
  183.0 18.2 %copy-start.5 = (f32[1,4096]{1,0:T(1,128)S(1)}, f32[1,4096]{1,0:T(1,128)}, u32[]{:S(2)}) copy-start(f32[1,4096]{1,0:T(1,128)} %copy-done.4) | copy-start | bytes 49156
  185.1 14.5 %collective-permute-start = (bf16[128,4096]{1,0:T(8,128)(2,1)}, bf16[128,4096]{1,0:T(8,128)(2,1)}, u32[]{:S(2)}, u32[]{:S(2)}) collective-permute-start(bf16[128,4096]{1,0:T(8,128)(2,1)} %fusion.3), channel_id=1, source_target_pairs={{0,16},{16,32},{32,48},{48,64},{64,80},{80,96},{96,112},{112,128},... | collective-permute-start | bytes 3145736 | tf_op jit(solution)/shard_map/ppermute | solution.py:12
  203.1 56.4 %copy-start.10 = (bf16[1,4096,384]{2,1,0:T(8,128)(2,1)S(1)}, bf16[1,4096,384]{2,1,0:T(8,128)(2,1)}, u32[]{:S(2)}) copy-start(bf16[1,4096,384]{2,1,0:T(8,128)(2,1)} %param.9) | copy-start | bytes 9437188
  258.2 1.3 copy-start.2
  267.7 99.8 %all-to-all-start.3 = ((f32[16,1,16,4096]{3,2,1,0:T(8,128)}), f32[16,1,16,4096]{3,2,1,0:T(8,128)}, u32[]{:S(2)}, u32[]{:S(2)}) async-start(f32[16,1,16,4096]{3,2,1,0:T(8,128)} %convolution_bitcast_fusion), calls=%async_computation.3 | async-start | bytes 8388608 | tf_op jit(solution)/shard_map/all_to_all | solution.py:53
where the time goes:
time: 375 us; the launch traced here: 373 us
  waiting for transfers between devices  206 us (55%)
  blocking collectives  119 us (32%)
  matrix products  25.3 us (7%)
  other arithmetic  9.74 us (3%)
  starting transfers between devices  9.19 us (2%)
  local copies, waits for them, and re-layouts  4.26 us (1%)
    all_to_all x2, waiting for transfers between devices, one_stop(): lax.all_to_all(jnp.einsum('skmh,khd->skmd', hidden, down_w, preferred_ele...  192 us
    all_to_all x2, blocking collectives, one_stop(): lax.all_to_all(outgoing, 'expert', split_axis=0, concat_axis=0, tiled=True)  119 us
    ppermute x1, waiting for transfers between devices, passed_along(): return lax.ppermute(value, axis, pairs)  14.2 us
    dot_general x2, matrix products, one_stop(): jnp.einsum('skmh,khd->skmd', hidden, down_w, preferred_element_type=jnp.f...  13.8 us
    all_to_all x2, starting transfers between devices, one_stop(): lax.all_to_all(jnp.einsum('skmh,khd->skmd', hidden, down_w, preferred_ele...  9.19 us
  transfers between devices with their start and end apart: 3, of which 3 were waited for; matrix products, arithmetic and copies ran while one was open for 0% of the time, Pallas kernels for 0%

commit v1 on v0

v1 whole, which is shorter than its diff:
```python
import functools

import jax
import jax.numpy as jnp
from jax import lax
from jax.experimental import pallas as pl
from jax.experimental.pallas import tpu as pltpu
from jax.sharding import PartitionSpec as P

MESH = pl.DeviceIdType.MESH
F32, BF16 = jnp.float32, jnp.bfloat16
POS = {0: 0, 4: 1, 1: 2, 5: 3, 2: 4, 6: 5, 3: 6, 7: 7}
CAP = 16
UP, MATE, CROSS, BACK, PAIR, LAST = 0, 4, 8, 16, 24, 28
CHANNELS = 32


def unit(u):
    return pl.ds(POS[u] * CAP, CAP)


def routing(ids, weights, experts):
    tokens = ids.shape[1]
    matched, factors = [], []
    for e in experts:
        hit = ids == e
        matched.append(jnp.max(jnp.where(hit, 1.0, 0.0), axis=0, keepdims=True))
        factors.append(jnp.sum(jnp.where(hit, weights, 0.0), axis=0, keepdims=True))
    named = jnp.concatenate(matched + matched, axis=0)
    earlier = lax.broadcasted_iota(jnp.int32, (tokens, tokens), 0) < lax.broadcasted_iota(
        jnp.int32, (tokens, tokens), 1
    )
    rank = jnp.dot(
        named.astype(BF16), jnp.where(earlier, 1.0, 0.0).astype(BF16), preferred_element_type=F32
    )
    slot = lax.broadcasted_iota(jnp.int32, (CAP, tokens), 0).astype(F32)
    select = [
        jnp.where(jnp.logical_and(rank[j : j + 1] == slot, matched[j] > 0.5), 1.0, 0.0)
        for j in range(4)
    ]
    coefs = jnp.concatenate([select[j] * factors[j] for j in range(4)], axis=0)
    return jnp.concatenate(select, axis=0).astype(BF16), coefs


def split_coefs(coefs):
    first = coefs.astype(BF16).astype(F32)
    second = (coefs - first).astype(BF16).astype(F32)
    third = coefs - first - second
    left = jnp.concatenate([first, second], axis=0).T
    right = jnp.concatenate([third, jnp.zeros_like(third)], axis=0).T
    return jnp.concatenate([left, right], axis=1).astype(BF16)


def kernel(
    act, gain, wg, wu, wd, ids, weights, out,
    tok, sel, coef, rows, sbuf, own, par, gu, hid, psend, pown, rx, ms, rz, fs, res, w1, w2, pids, pwts,
    ssem, rsem, hs, hr, lsem,
):
    s, k = lax.axis_index("section"), lax.axis_index("expert")
    sections = lax.axis_size("section")
    z, h = k // 2, lax.rem(k, 2)
    b = lax.rem(z, 2)
    dr = 2 * b - 1
    p = z // 2
    width = tok.shape[2]
    hidden = wd.shape[0]
    nxt, prv = lax.rem(s + 1, sections), lax.rem(s + sections - 1, sections)

    def at(dz=0, cross=False, section=None):
        there = lax.rem(z + dz + 8, 8) * 2 + (1 - h if cross else h)
        return (s if section is None else section, there)

    loads = [
        pltpu.make_async_copy(act, tok.at[0], lsem.at[0]),
        pltpu.make_async_copy(wg, w1.at[:, pl.ds(0, hidden)], lsem.at[1]),
        pltpu.make_async_copy(wu, w1.at[:, pl.ds(hidden, hidden)], lsem.at[2]),
        pltpu.make_async_copy(wd, w2, lsem.at[3]),
    ]
    for load in loads:
        load.start()

    barrier = pltpu.get_barrier_semaphore()
    near = [at(dr), at(2 * dr), at(-2 * dr), at(3 * dr), at(-dr), at(0, cross=True)]
    below = [at(j, section=prv) for j in (0, dr, -2 * dr, 3 * dr)]
    for device in near + below:
        pl.semaphore_signal(barrier, inc=1, device_id=device, device_id_type=MESH)
    pl.semaphore_wait(barrier, len(near) + 4)

    def remote(src, dst, send, recv, device):
        return pltpu.make_async_remote_copy(
            src_ref=src, dst_ref=dst, send_sem=send, recv_sem=recv, device_id=device, device_id_type=MESH
        )

    handoff = [
        remote(ids.at[0], pids, hs.at[0], hr.at[0], at(section=nxt)),
        remote(weights.at[0], pwts, hs.at[1], hr.at[1], at(section=nxt)),
        remote(act, tok.at[1], hs.at[2], hr.at[2], at(section=nxt)),
    ]
    for copy in handoff:
        copy.start()

    experts = (p, lax.rem(p + dr + 4, 4), lax.rem(p - dr + 4, 4), lax.rem(p + 2, 4))
    sel[0] = routing(ids[0], weights[0], experts)[0]
    loads[0].wait()

    def prologue(r):
        def pick(n, total):
            cols = pl.ds(pl.multiple_of(n * 512, 512), 512)
            block = jnp.dot(sel[r], tok[2 * r, :, cols], preferred_element_type=F32)
            rows[:, cols] = block
            square = block * block
            return total + square[:, :128] + square[:, 128:256] + square[:, 256:384] + square[:, 384:]

        total = lax.fori_loop(0, width // 512, pick, jnp.zeros((4 * CAP, 128), F32))
        scale = lax.rsqrt(jnp.sum(total, axis=1, keepdims=True) * (1.0 / width) + 1e-06)

        @pl.loop(0, width // 512)
        def _(n):
            cols = pl.ds(pl.multiple_of(n * 512, 512), 512)
            block = (rows[:, cols] * scale * gain[:, cols].astype(F32)).astype(BF16)
            own[r, unit(0), cols] = block[:CAP]
            for j in range(1, 4):
                sbuf[r, j, :, cols] = block[j * CAP : (j + 1) * CAP]

    def epilogue(r, put):
        @pl.loop(0, width // 512)
        def _(n):
            cols = pl.ds(pl.multiple_of(n * 512, 512), 512)
            block = res[r, :, cols]
            mixed = jnp.dot(
                coef[r], jnp.concatenate([block] * 4, axis=0), preferred_element_type=F32
            )
            put(cols, (tok[1 + r, :, cols].astype(F32) + mixed).astype(BF16))

    def ffn(r, table, start, count, dst):
        chunk = pl.ds(start, count)

        @pl.loop(0, (2 * hidden) // 256)
        def _(n):
            cols = pl.ds(pl.multiple_of(n * 256, 256), 256)
            gu[pl.ds(0, count), cols] = jnp.dot(
                table[r, chunk, :], w1[:, cols], preferred_element_type=F32
            )

        gate, up = gu[pl.ds(0, count), pl.ds(0, hidden)], gu[pl.ds(0, count), pl.ds(hidden, hidden)]
        hid[pl.ds(0, count), :] = (gate / (1.0 + jnp.exp(-gate)) * up).astype(BF16)

        @pl.loop(0, width // 512)
        def _(n):
            cols = pl.ds(pl.multiple_of(n * 512, 512), 512)
            dst[r, chunk, cols] = jnp.dot(
                hid[pl.ds(0, count), :], w2[:, cols], preferred_element_type=F32
            ).astype(dst.dtype)

    started = []
    for r in range(2):

        def channel(src, dst, index, device):
            copy = remote(src, dst, ssem.at[r, index], rsem.at[r, index], device)
            return copy

        up = {
            j: channel(sbuf.at[r, j], own.at[r, unit(j)], UP + j, at(d))
            for j, d in ((1, dr), (2, -2 * dr), (3, 3 * dr))
        }
        mate = {
            j: channel(own.at[r, unit(j)], own.at[r, unit(4 + j)], MATE + j, at(-dr))
            for j in range(4)
        }
        cross = {
            u: channel(own.at[r, unit(u)], par.at[r, unit(u)], CROSS + u, at(0, cross=True))
            for u in range(8)
        }
        back = {
            u: channel(psend.at[r, unit(u)], rx.at[r, unit(u)], BACK + u, at(0, cross=True))
            for u in range(8)
        }
        pair = {
            j: channel(ms.at[r, j], rz.at[r, j], PAIR + j, at(-dr)) for j in range(4)
        }
        target = nxt if r == 0 else s
        last = {
            j: channel(
                fs.at[r, j],
                res.at[r, pl.ds(j * CAP, CAP)],
                LAST + j,
                at(dr * j, section=target),
            )
            for j in range(4)
            if r == 0 or j > 0
        }

        def go(copy):
            copy.start()
            started.append(copy)

        prologue(r)
        go(cross[0])
        go(mate[0])
        for j in (3, 2, 1):
            go(up[j])
        if r == 0:
            sel[1], coefs = routing(ids[1], weights[1], experts)
            coef[1] = split_coefs(coefs)
            handoff[0].wait_recv()
            handoff[1].wait_recv()
            coef[0] = split_coefs(routing(pids[...], pwts[...], experts)[1])
        for u in (4, 1, 5, 2, 6, 3, 7):
            if u < 4:
                up[u].wait_recv()
                go(mate[u])
            else:
                mate[u - 4].wait_recv()
            go(cross[u])
        if r == 0:
            for load in loads[1:]:
                load.wait()
        ffn(r, own, 0, 8 * CAP, pown)
        for half, order in ((0, (5, 4, 1, 0)), (1, (7, 6, 3, 2))):
            for u in order:
                cross[u].wait_recv()
            ffn(r, par, half * 4 * CAP, 4 * CAP, psend)
            for u in order:
                go(back[u])

        for first, second in ((1, 0), (3, 2)):
            for j in (first, second):
                back[4 + j].wait_recv()
                ms[r, j] = (pown[r, unit(4 + j), :] + rx[r, unit(4 + j), :].astype(F32)).astype(BF16)
                go(pair[j])
            for j in (first, second):
                back[j].wait_recv()
                pair[j].wait_recv()
                total = (
                    pown[r, unit(j), :] + rx[r, unit(j), :].astype(F32) + rz[r, j].astype(F32)
                ).astype(BF16)
                if j in last:
                    fs[r, j] = total
                    go(last[j])
                else:
                    res[r, pl.ds(j * CAP, CAP), :] = total
        for copy in last.values():
            copy.wait_recv()
        if r == 0:
            handoff[2].wait_recv()

            def keep(cols, block):
                tok[2, :, cols] = block
        else:

            def keep(cols, block):
                out[:, cols] = block

        epilogue(r, keep)

    for copy in started + handoff:
        copy.wait_send()


def body(activations, norm_gain, w_gate, w_up, w_down, expert_ids, route_weights):
    tokens, width = activations.shape[1:]
    hidden = w_gate.shape[2]
    slots = 4 * CAP
    anywhere = pl.BlockSpec(memory_space=pl.ANY)
    vmem = pl.BlockSpec(memory_space=pltpu.VMEM)
    out = pl.pallas_call(
        kernel,
        out_shape=jax.ShapeDtypeStruct((tokens, width), BF16),
        in_specs=[anywhere, vmem, anywhere, anywhere, anywhere, vmem, vmem],
        out_specs=vmem,
        scratch_shapes=[
            pltpu.VMEM((3, tokens, width), BF16),
            pltpu.VMEM((2, slots, tokens), BF16),
            pltpu.VMEM((2, tokens, 4 * slots), BF16),
            pltpu.VMEM((slots, width), F32),
            pltpu.VMEM((2, 4, CAP, width), BF16),
            pltpu.VMEM((2, 8 * CAP, width), BF16),
            pltpu.VMEM((2, 8 * CAP, width), BF16),
            pltpu.VMEM((8 * CAP, 2 * hidden), F32),
            pltpu.VMEM((8 * CAP, hidden), BF16),
            pltpu.VMEM((2, 8 * CAP, width), BF16),
            pltpu.VMEM((2, 8 * CAP, width), F32),
            pltpu.VMEM((2, 8 * CAP, width), BF16),
            pltpu.VMEM((2, 4, CAP, width), BF16),
            pltpu.VMEM((2, 4, CAP, width), BF16),
            pltpu.VMEM((2, 4, CAP, width), BF16),
            pltpu.VMEM((2, slots, width), BF16),
            pltpu.VMEM((width, 2 * hidden), BF16),
            pltpu.VMEM((hidden, width), BF16),
            pltpu.VMEM((8, tokens), jnp.int32),
            pltpu.VMEM((8, tokens), F32),
            pltpu.SemaphoreType.DMA((2, CHANNELS)),
            pltpu.SemaphoreType.DMA((2, CHANNELS)),
            pltpu.SemaphoreType.DMA((3,)),
            pltpu.SemaphoreType.DMA((3,)),
            pltpu.SemaphoreType.DMA((4,)),
        ],
        compiler_params=pltpu.CompilerParams(
            collective_id=0, has_side_effects=True, vmem_limit_bytes=56 << 20
        ),
        cost_estimate=pl.CostEstimate(
            flops=12 * 256 * width * hidden, bytes_accessed=12 << 20, transcendentals=512 * hidden
        ),
    )(
        activations[0],
        norm_gain,
        w_gate[0],
        w_up[0],
        w_down[0],
        jnp.swapaxes(expert_ids[:, 0], 1, 2),
        jnp.swapaxes(route_weights[:, 0], 1, 2),
    )
    return out[None]


def solution(mesh):
    return jax.shard_map(
        body,
        mesh=mesh,
        in_specs=(
            P("section", "expert", None),
            P("section", None),
            P("section", None, "expert"),
            P("section", None, "expert"),
            P("section", "expert", None),
            P(None, "section", "expert", None),
            P(None, "section", "expert", None),
        ),
        out_specs=P("section", "expert", None),
        check_vma=False,
    )
```

time: 375 us -> 149 us (0.40)
  waiting for transfers between devices: 206 us -> 0 us
  Pallas kernels: 0 us -> 147 us
  blocking collectives: 119 us -> 0 us
  matrix products: 25.3 us -> 0 us
  other arithmetic: 9.74 us -> 0 us
  starting transfers between devices: 9.19 us -> 0 us
    all_to_all x2 -> x0, waiting for transfers between devices: 192 us -> none  [one_stop(): lax.all_to_all(jnp.einsum('skmh,khd->skmd', hidden, down_w, preferred_ele...]
    pallas_call x0 -> x1, Pallas kernels: none -> 147 us  [body(): pl.pallas_call(kernel, out_shape=jax.ShapeDtypeStruct((tokens, width), BF...]
    all_to_all x2 -> x0, blocking collectives: 119 us -> none  [one_stop(): lax.all_to_all(outgoing, 'expert', split_axis=0, concat_axis=0, tiled=True)]
    dot_general x8 -> x0, matrix products: 25.3 us -> none  [the longest x2 13.8 us: one_stop(): jnp.einsum('skmh,khd->skmd', hidden, down_w, preferred_element_type=jnp.f...]
    ppermute x1 -> x0, waiting for transfers between devices: 14.2 us -> none  [passed_along(): return lax.ppermute(value, axis, pairs)]
    all_to_all x2 -> x0, starting transfers between devices: 9.19 us -> none  [one_stop(): lax.all_to_all(jnp.einsum('skmh,khd->skmd', hidden, down_w, preferred_ele...]
    reduce_sum x6 -> x0, other arithmetic: 8.57 us -> none  [the longest x2 5.35 us: one_stop(): jnp.sum(partials.reshape(groups, group_size, per_device, capacity, model_...]
  transfers between devices with their start and end apart: 3 -> 0, of which waited for: 3 -> 0; matrix products, arithmetic and copies ran while one was open for 0% -> 0% of each run, Pallas kernels for 0% -> 0%
where the time goes in v1:
time: 149 us
  Pallas kernels  147 us (99%)
  local copies, waits for them, and re-layouts  2.29 us (2%)
    pallas_call x1, Pallas kernels, body(): pl.pallas_call(kernel, out_shape=jax.ShapeDtypeStruct((tokens, width), BF...  147 us

profile of v1, /device:TPU:24, one launch (start us, length us, event | category | flops | bytes accessed | tf_op | source)
XLA Modules:
  0.0 149.0 jit_solution(13435120619199560433)
XLA Ops:
  0.0 146.7 %shard_map.73 = bf16[128,4096]{1,0:T(8,128)(2,1)} custom-call(bf16[128,4096]{1,0:T(8,128)(2,1)} %bitcast.15, bf16[1,4096]{1,0:T(2,128)(2,1)} %gain.1, bf16[4096,384]{1,0:T(8,128)(2,1)} %bitcast.12, bf16[4096,384]{1,0:T(8,128)(2,1)} %bitcast.13, bf16[384,4096]{1,0:T(8,128)(2,1)} %bitcast.14, s32[2,8,128]{2,1,0:T(8,128)} %bitcast.16, f32[2,8,128]{2,1,0:T(8,128)} %bitcast.17), custom_call_target="tpu_custom_call" | custom-call | flops 4831838208 | bytes 12582912 | tf_op jit(solution)/shard_map/pallas_call | solution.py:266
  146.7 2.3 %copy.9 = bf16[1,128,4096]{2,1,0:T(8,128)(2,1)} copy(bf16[1,128,4096]{2,1,0:T(8,128)(2,1)} %bitcast.11) | data formatting | bytes 2097152

commit v2 on v1

v2 whole, which is shorter than its diff:
```python
import functools

import jax
import jax.numpy as jnp
from jax import lax
from jax.experimental import pallas as pl
from jax.experimental.pallas import tpu as pltpu
from jax.sharding import PartitionSpec as P

MESH = pl.DeviceIdType.MESH
F32, BF16 = jnp.float32, jnp.bfloat16
POS = {0: 0, 4: 1, 1: 2, 5: 3, 2: 4, 6: 5, 3: 6, 7: 7}
CAP = 16
UP, MATE, CROSS, BACK, PAIR, LAST = 0, 4, 8, 16, 24, 28
CHANNELS = 32


def unit(u):
    return pl.ds(POS[u] * CAP, CAP)


def routing(ids, weights, experts):
    tokens = ids.shape[1]
    matched, factors = [], []
    for e in experts:
        hit = ids == e
        matched.append(jnp.max(jnp.where(hit, 1.0, 0.0), axis=0, keepdims=True))
        factors.append(jnp.sum(jnp.where(hit, weights, 0.0), axis=0, keepdims=True))
    named = jnp.concatenate(matched + matched, axis=0)
    earlier = lax.broadcasted_iota(jnp.int32, (tokens, tokens), 0) < lax.broadcasted_iota(
        jnp.int32, (tokens, tokens), 1
    )
    rank = jnp.dot(
        named.astype(BF16), jnp.where(earlier, 1.0, 0.0).astype(BF16), preferred_element_type=F32
    )
    slot = lax.broadcasted_iota(jnp.int32, (CAP, tokens), 0).astype(F32)
    select = [
        jnp.where(jnp.logical_and(rank[j : j + 1] == slot, matched[j] > 0.5), 1.0, 0.0)
        for j in range(4)
    ]
    coefs = jnp.concatenate([select[j] * factors[j] for j in range(4)], axis=0)
    return jnp.concatenate(select, axis=0).astype(BF16), coefs


def split_coefs(coefs):
    first = coefs.astype(BF16).astype(F32)
    second = (coefs - first).astype(BF16).astype(F32)
    third = coefs - first - second
    left = jnp.concatenate([first, second], axis=0).T
    right = jnp.concatenate([third, jnp.zeros_like(third)], axis=0).T
    return jnp.concatenate([left, right], axis=1).astype(BF16)


def combine(coefs, results, carried):
    mixed = jnp.dot(coefs, jnp.concatenate([results] * 4, axis=0), preferred_element_type=F32)
    return (carried.astype(F32) + mixed).astype(BF16)


def last_step(coefs, results, carried, out, c, r, t, o, sems, osems):
    step = r.shape[2]
    loads = [pltpu.make_async_copy(coefs, c, sems.at[0])]
    for n in range(r.shape[0]):
        cols = pl.ds(n * step, step)
        loads.append(pltpu.make_async_copy(results.at[:, cols], r.at[n], sems.at[2 * n + 1]))
        loads.append(pltpu.make_async_copy(carried.at[:, cols], t.at[n], sems.at[2 * n + 2]))
    for load in loads:
        load.start()
    loads[0].wait()
    stores = []
    for n in range(r.shape[0]):
        loads[2 * n + 1].wait()
        loads[2 * n + 2].wait()
        o[n] = combine(c[...], r[n], t[n])
        stores.append(pltpu.make_async_copy(o.at[n], out.at[0, :, pl.ds(n * step, step)], osems.at[n]))
        stores[n].start()
    for store in stores:
        store.wait()


def kernel(
    act, gain, wg, wu, wd, ids, weights, base, results, coefs1,
    tok, sel, coef, rows, sbuf, own, par, gu, hid, psend, pown, rx, ms, rz, fs, res, w1, w2, pids, pwts,
    relay, ppr, ssem, rsem, hs, hr, lsem,
):
    s, k = lax.axis_index("section"), lax.axis_index("expert")
    sections = lax.axis_size("section")
    z, h = k // 2, lax.rem(k, 2)
    b = lax.rem(z, 2)
    dr = 2 * b - 1
    p = z // 2
    width = tok.shape[2]
    hidden = wd.shape[0]
    nxt, prv = lax.rem(s + 1, sections), lax.rem(s + sections - 1, sections)

    def at(dz=0, cross=False, section=None):
        there = lax.rem(z + dz + 8, 8) * 2 + (1 - h if cross else h)
        return (s if section is None else section, there)

    loads = [
        pltpu.make_async_copy(act, tok.at[0], lsem.at[0]),
        pltpu.make_async_copy(wg, w1.at[:, pl.ds(0, hidden)], lsem.at[1]),
        pltpu.make_async_copy(wu, w1.at[:, pl.ds(hidden, hidden)], lsem.at[2]),
        pltpu.make_async_copy(wd, w2, lsem.at[3]),
    ]
    for load in loads:
        load.start()
    keep_coefs = pltpu.make_async_copy(coef.at[1], coefs1, lsem.at[4])
    keep_base = pltpu.make_async_copy(tok.at[2], base, lsem.at[5])

    barrier = pltpu.get_barrier_semaphore()
    near = [at(dr), at(2 * dr), at(-2 * dr), at(3 * dr), at(-dr), at(0, cross=True)]
    below = [at(j, section=prv) for j in (0, dr, -2 * dr, 3 * dr)]
    for device in near + below:
        pl.semaphore_signal(barrier, inc=1, device_id=device, device_id_type=MESH)

    side, y, core = s // 8, lax.rem(s // 2, 4), lax.rem(s, 2)
    tail, head = side * 8 + 7, (1 - side) * 8
    is_tail = jnp.logical_and(y == 3, core == 1)
    is_head = jnp.logical_and(y == 0, core == 0)
    before = jnp.logical_and(y < 3, core == 1)
    after = jnp.logical_and(y > 0, core == 0)

    def greet(section):
        pl.semaphore_signal(barrier, inc=1, device_id=at(section=section), device_id_type=MESH)

    @pl.when(before)
    def _():
        greet(tail)

    @pl.when(after)
    def _():
        greet(jnp.where(y == 3, head + 7, head + 2 * y + 1))

    @pl.when(is_head)
    def _():
        greet(head + 1)
        for q in (1, 2, 3):
            greet(side * 8 + 2 * q)

    more = jnp.where(is_tail, 4, jnp.where(is_head, 0, 1))

    def remote(src, dst, send, recv, device):
        return pltpu.make_async_remote_copy(
            src_ref=src, dst_ref=dst, send_sem=send, recv_sem=recv, device_id=device, device_id_type=MESH
        )

    handoff = [
        remote(ids.at[0], pids, hs.at[0], hr.at[0], at(section=nxt)),
        remote(weights.at[0], pwts, hs.at[1], hr.at[1], at(section=nxt)),
    ]
    whole = remote(act, tok.at[1], hs.at[2], hr.at[2], at(section=nxt))

    def quarter(q):
        return pl.ds(q * 2 * CAP, 2 * CAP)

    parts = [
        remote(
            act.at[quarter(q)], relay, hs.at[3 + q], hr.at[3],
            at(section=side * 8 + 2 * q + 1 if q < 3 else head + 6),
        )
        for q in range(4)
    ]
    over = remote(relay, relay, hs.at[7], hr.at[3], at(section=head + 2 * y))
    over_last = remote(relay, tok.at[1, quarter(0)], hs.at[7], hr.at[4], at(section=head))
    home = [
        remote(relay, tok.at[1, quarter(q)], hs.at[7], hr.at[4 + q], at(section=side * 8))
        for q in range(1, 4)
    ]

    def handoff_start():
        @pl.when(is_tail)
        def _():
            for copy in parts:
                copy.start()

        @pl.when(jnp.logical_not(is_tail))
        def _():
            whole.start()

    def handoff_over():
        @pl.when(before)
        def _():
            over.wait_recv()

            @pl.when(y == 0)
            def _():
                over_last.start()

            @pl.when(y > 0)
            def _():
                over.start()

    def handoff_home():
        @pl.when(after)
        def _():
            over.wait_recv()
            for q in range(1, 4):

                @pl.when(y == q)
                def _():
                    home[q - 1].start()

    def handoff_arrived():
        @pl.when(is_head)
        def _():
            over_last.wait_recv()
            for copy in home:
                copy.wait_recv()

        @pl.when(jnp.logical_not(is_head))
        def _():
            whole.wait_recv()

    def handoff_sent():
        @pl.when(is_tail)
        def _():
            for copy in parts:
                copy.wait_send()

        @pl.when(jnp.logical_not(is_tail))
        def _():
            whole.wait_send()

        @pl.when(jnp.logical_or(before, after))
        def _():
            over.wait_send()
    experts = (p, lax.rem(p + dr + 4, 4), lax.rem(p - dr + 4, 4), lax.rem(p + 2, 4))
    sel[0] = routing(ids[0], weights[0], experts)[0]
    loads[0].wait()

    def prologue(r):
        total = jnp.zeros((4 * CAP, 128), F32)
        for n in range(0, width, 1024):
            cols = pl.ds(n, 1024)
            block = jnp.dot(sel[r], tok[2 * r, :, cols], preferred_element_type=F32)
            rows[:, cols] = block
            for m in range(0, 1024, 128):
                total += block[:, m : m + 128] * block[:, m : m + 128]
        scale = lax.rsqrt(jnp.sum(total, axis=1, keepdims=True) * (1.0 / width) + 1e-06)
        for n in range(0, width, 1024):
            cols = pl.ds(n, 1024)
            block = (rows[:, cols] * scale * gain[:, cols].astype(F32)).astype(BF16)
            own[r, unit(0), cols] = block[:CAP]
            for j in range(1, 4):
                sbuf[r, j, :, cols] = block[j * CAP : (j + 1) * CAP]

    def epilogue():
        for n in range(0, width, 1024):
            cols = pl.ds(n, 1024)
            tok[2, :, cols] = combine(coef[0], res[:, cols], tok[1, :, cols])

    def ffn(r, table, start, count, dst):
        chunk = pl.ds(start, count)

        @pl.loop(0, (2 * hidden) // 256)
        def _(n):
            cols = pl.ds(pl.multiple_of(n * 256, 256), 256)
            gu[pl.ds(0, count), cols] = jnp.dot(
                table[r, chunk, :], w1[:, cols], preferred_element_type=F32
            )

        gate, up = gu[pl.ds(0, count), pl.ds(0, hidden)], gu[pl.ds(0, count), pl.ds(hidden, hidden)]
        hid[pl.ds(0, count), :] = (gate / (1.0 + jnp.exp(-gate)) * up).astype(BF16)

        for n in range(0, width, 1024):
            cols = pl.ds(n, 1024)
            block = jnp.dot(hid[pl.ds(0, count), :], w2[:, cols], preferred_element_type=F32)
            if dst is pown:
                dst[chunk, cols] = block
            else:
                dst[r, chunk, cols] = block.astype(BF16)

    started = []
    for r in range(2):

        def channel(src, dst, index, device):
            copy = remote(src, dst, ssem.at[r, index], rsem.at[r, index], device)
            return copy

        up = {
            j: channel(sbuf.at[r, j], own.at[r, unit(j)], UP + j, at(d))
            for j, d in ((1, dr), (2, -2 * dr), (3, 3 * dr))
        }
        mate = {
            j: channel(own.at[r, unit(j)], own.at[r, unit(4 + j)], MATE + j, at(-dr))
            for j in range(4)
        }
        cross = {
            u: channel(own.at[r, unit(u)], par.at[r, unit(u)], CROSS + u, at(0, cross=True))
            for u in (0, 1, 2, 3, 5, 6, 7)
        }
        cross[4] = channel(par.at[r, unit(0)], par.at[r, unit(4)], CROSS + 4, at(-dr))
        back = {
            u: channel(psend.at[r, unit(u)], rx.at[r, unit(u)], BACK + u, at(0, cross=True))
            for u in (0, 1, 2, 3, 5, 6, 7)
        }
        back[4] = channel(psend.at[r, unit(4)], ppr.at[r], BACK + 4, at(-dr))
        pair = {
            j: channel(ms.at[r, j], rz.at[r, j], PAIR + j, at(-dr)) for j in range(4)
        }
        dest, target = (res, nxt) if r == 0 else (results, s)
        last = {
            j: channel(
                fs.at[r, j], dest.at[pl.ds(j * CAP, CAP)], LAST + j, at(dr * j, section=target)
            )
            for j in range(r, 4)
        }
        if r == 1:
            last[0] = pltpu.make_async_copy(
                fs.at[r, 0], results.at[pl.ds(0, CAP)], rsem.at[r, LAST]
            )

        def go(copy, tracked=True):
            copy.start()
            if tracked:
                started.append(copy)

        prologue(r)
        if r == 0:
            pl.semaphore_wait(barrier, len(near) + len(below) + more)
        go(cross[0])
        go(mate[0])
        go(up[1])
        go(up[3])
        go(up[2])
        if r == 0:
            for copy in handoff:
                copy.start()
            handoff_start()
            sel[1], coefs = routing(ids[1], weights[1], experts)
            coef[1] = split_coefs(coefs)
            keep_coefs.start()
            for load in loads[1:]:
                load.wait()
        mate[0].wait_recv()
        up[1].wait_recv()
        go(mate[1])
        go(cross[1])
        cross[0].wait_recv()
        go(cross[4])
        mate[1].wait_recv()
        go(cross[5])
        for j in (3, 2):
            up[j].wait_recv()
            go(mate[j])
            go(cross[j])
            mate[j].wait_recv()
            go(cross[4 + j])
        for u in (4, 1, 5):
            cross[u].wait_recv()
        ffn(r, par, 0, 4 * CAP, psend)
        go(back[5])
        go(back[1])
        go(back[4])
        if r == 0:
            handoff_over()
        ffn(r, own, 0, 8 * CAP, pown)
        ms[r, 0] = pown[unit(4), :].astype(BF16)
        go(pair[0])
        for u in (2, 6, 3, 7):
            cross[u].wait_recv()
        ffn(r, par, 4 * CAP, 4 * CAP, psend)
        for u in (7, 3, 6, 2):
            go(back[u])
        back[4].wait_recv()
        psend[r, unit(0), :] = (psend[r, unit(0), :].astype(F32) + ppr[r].astype(F32)).astype(BF16)
        go(back[0])
        if r == 0:
            handoff[0].wait_recv()
            handoff[1].wait_recv()
            coef[0] = split_coefs(routing(pids[...], pwts[...], experts)[1])

        def toward_mate(j):
            back[4 + j].wait_recv()
            ms[r, j] = (pown[unit(4 + j), :] + rx[r, unit(4 + j), :].astype(F32)).astype(BF16)
            go(pair[j])

        def finish(j):
            back[j].wait_recv()
            pair[j].wait_recv()
            fs[r, j] = (
                pown[unit(j), :] + rx[r, unit(j), :].astype(F32) + rz[r, j].astype(F32)
            ).astype(BF16)
            go(last[j], tracked=r == 0 or j > 0)

        toward_mate(1)
        toward_mate(3)
        finish(1)
        toward_mate(2)
        if r == 0:
            handoff_home()
        finish(3)

        finish(2)
        finish(0)
        if r == 0:
            for j in (1, 3, 2, 0):
                last[j].wait_recv()
            handoff_arrived()
            epilogue()
            keep_base.start()
        else:
            for j in (1, 3, 2):
                last[j].wait_recv()
            last[0].wait()

    keep_coefs.wait()
    keep_base.wait()
    for copy in started + handoff:
        copy.wait_send()
    handoff_sent()


def body(activations, norm_gain, w_gate, w_up, w_down, expert_ids, route_weights):
    tokens, width = activations.shape[1:]
    hidden = w_gate.shape[2]
    slots = 4 * CAP
    anywhere = pl.BlockSpec(memory_space=pl.ANY)
    vmem = pl.BlockSpec(memory_space=pltpu.VMEM)
    base, results, coefs = pl.pallas_call(
        kernel,
        out_shape=[
            jax.ShapeDtypeStruct((tokens, width), BF16),
            jax.ShapeDtypeStruct((slots, width), BF16),
            jax.ShapeDtypeStruct((tokens, 4 * slots), BF16),
        ],
        in_specs=[anywhere, vmem, anywhere, anywhere, anywhere, vmem, vmem],
        out_specs=[anywhere, anywhere, anywhere],
        scratch_shapes=[
            pltpu.VMEM((3, tokens, width), BF16),
            pltpu.VMEM((2, slots, tokens), BF16),
            pltpu.VMEM((2, tokens, 4 * slots), BF16),
            pltpu.VMEM((slots, width), F32),
            pltpu.VMEM((2, 4, CAP, width), BF16),
            pltpu.VMEM((2, 8 * CAP, width), BF16),
            pltpu.VMEM((2, 8 * CAP, width), BF16),
            pltpu.VMEM((8 * CAP, 2 * hidden), F32),
            pltpu.VMEM((8 * CAP, hidden), BF16),
            pltpu.VMEM((2, 8 * CAP, width), BF16),
            pltpu.VMEM((8 * CAP, width), F32),
            pltpu.VMEM((2, 8 * CAP, width), BF16),
            pltpu.VMEM((2, 4, CAP, width), BF16),
            pltpu.VMEM((2, 4, CAP, width), BF16),
            pltpu.VMEM((2, 4, CAP, width), BF16),
            pltpu.VMEM((slots, width), BF16),
            pltpu.VMEM((width, 2 * hidden), BF16),
            pltpu.VMEM((hidden, width), BF16),
            pltpu.VMEM((8, tokens), jnp.int32),
            pltpu.VMEM((8, tokens), F32),
            pltpu.VMEM((2 * CAP, width), BF16),
            pltpu.VMEM((2, CAP, width), BF16),
            pltpu.SemaphoreType.DMA((2, CHANNELS)),
            pltpu.SemaphoreType.DMA((2, CHANNELS)),
            pltpu.SemaphoreType.DMA((8,)),
            pltpu.SemaphoreType.DMA((8,)),
            pltpu.SemaphoreType.DMA((6,)),
        ],
        compiler_params=pltpu.CompilerParams(
            collective_id=0, has_side_effects=True, vmem_limit_bytes=56 << 20
        ),
        cost_estimate=pl.CostEstimate(
            flops=12 * 256 * width * hidden, bytes_accessed=12 << 20, transcendentals=512 * hidden
        ),
    )(
        activations[0],
        norm_gain,
        w_gate[0],
        w_up[0],
        w_down[0],
        jnp.swapaxes(expert_ids[:, 0], 1, 2),
        jnp.swapaxes(route_weights[:, 0], 1, 2),
    )
    step = 1024
    pieces = width // step
    return pl.pallas_call(
        last_step,
        out_shape=jax.ShapeDtypeStruct((1, tokens, width), BF16),
        in_specs=[anywhere] * 3,
        out_specs=anywhere,
        scratch_shapes=[
            pltpu.VMEM((tokens, 4 * slots), BF16),
            pltpu.VMEM((pieces, slots, step), BF16),
            pltpu.VMEM((pieces, tokens, step), BF16),
            pltpu.VMEM((pieces, tokens, step), BF16),
            pltpu.SemaphoreType.DMA((2 * pieces + 1,)),
            pltpu.SemaphoreType.DMA((pieces,)),
        ],
        compiler_params=pltpu.CompilerParams(vmem_limit_bytes=56 << 20),
    )(coefs, results, base)


def solution(mesh):
    return jax.shard_map(
        body,
        mesh=mesh,
        in_specs=(
            P("section", "expert", None),
            P("section", None),
            P("section", None, "expert"),
            P("section", None, "expert"),
            P("section", "expert", None),
            P(None, "section", "expert", None),
            P(None, "section", "expert", None),
        ),
        out_specs=P("section", "expert", None),
        check_vma=False,
    )
```

time: 149 us -> 131 us (0.88); the launches traced: 149 us -> 129 us
  Pallas kernels: 147 us -> 129 us
  local copies, waits for them, and re-layouts: 2.29 us -> 0 us
    pallas_call x1 -> x2, Pallas kernels: 147 us -> 129 us  [the longest x1 126 us: body(): pl.pallas_call(kernel, out_shape=[jax.ShapeDtypeStruct((tokens, width), B...]
    unnamed x1 -> x0, local copies, waits for them, and re-layouts: 2.29 us -> none
where the time goes in v2:
time: 131 us; the launch traced here: 129 us
  Pallas kernels  129 us (98%)
    pallas_call x1, Pallas kernels, body(): pl.pallas_call(kernel, out_shape=[jax.ShapeDtypeStruct((tokens, width), B...  126 us
    pallas_call x1, Pallas kernels, body(): pl.pallas_call(last_step, out_shape=jax.ShapeDtypeStruct((1, tokens, widt...  2.83 us

profile of v2, /device:TPU:24, one launch (start us, length us, event | category | flops | bytes accessed | tf_op | source)
XLA Modules:
  0.0 129.3 jit_solution(1760007602375224713)
XLA Ops:
  0.0 126.5 %shard_map.73 = (bf16[128,4096]{1,0:T(8,128)(2,1)}, bf16[64,4096]{1,0:T(8,128)(2,1)}, bf16[128,256]{1,0:T(8,128)(2,1)}) custom-call(bf16[128,4096]{1,0:T(8,128)(2,1)} %bitcast.13, bf16[1,4096]{1,0:T(2,128)(2,1)} %gain.1, bf16[4096,384]{1,0:T(8,128)(2,1)} %bitcast.10, bf16[4096,384]{1,0:T(8,128)(2,1)} %bitcast.11, bf16[384,4096]{1,0:T(8,128)(2,1)} %bitcast.12, ...), custom_call_target="tpu_custom_call" | custom-call | flops 4831838208 | bytes 12582912 | tf_op jit(solution)/shard_map/pallas_call | solution.py:420
  126.5 2.8 %shard_map.74 = bf16[1,128,4096]{2,1,0:T(8,128)(2,1)} custom-call(bf16[128,256]{1,0:T(8,128)(2,1)} %get-tuple-element.8.coefs, bf16[64,4096]{1,0:T(8,128)(2,1)} %get-tuple-element.9.results, bf16[128,4096]{1,0:T(8,128)(2,1)} %get-tuple-element.10.carried), custom_call_target="tpu_custom_call" | custom-call | tf_op jit(solution)/shard_map/pallas_call | solution.py:475

commit v3 on v2

--- a/solution.py
+++ b/solution.py
@@ -13,6 +13,8 @@
 CAP = 16
 UP, MATE, CROSS, BACK, PAIR, LAST = 0, 4, 8, 16, 24, 28
 CHANNELS = 32
+PIECES = 2
+BEHIND = 3
 
 
 def unit(u):
@@ -271,11 +273,20 @@
                 dst[r, chunk, cols] = block.astype(BF16)
 
     started = []
+
+    def piece(q):
+        return pl.ds(q * (width // PIECES), width // PIECES)
+
     for r in range(2):
 
         def channel(src, dst, index, device):
-            copy = remote(src, dst, ssem.at[r, index], rsem.at[r, index], device)
-            return copy
+            return [
+                remote(
+                    src.at[:, piece(q)], dst.at[:, piece(q)],
+                    ssem.at[r, index * PIECES + q], rsem.at[r, index * PIECES + q], device,
+                )
+                for q in range(PIECES)
+            ]
 
         up = {
             j: channel(sbuf.at[r, j], own.at[r, unit(j)], UP + j, at(d))
@@ -306,23 +317,33 @@
             for j in range(r, 4)
         }
         if r == 1:
-            last[0] = pltpu.make_async_copy(
-                fs.at[r, 0], results.at[pl.ds(0, CAP)], rsem.at[r, LAST]
-            )
-
-        def go(copy, tracked=True):
-            copy.start()
-            if tracked:
-                started.append(copy)
+            last[0] = [
+                pltpu.make_async_copy(
+                    fs.at[r, 0, :, piece(q)],
+                    results.at[pl.ds(0, CAP), piece(q)],
+                    rsem.at[r, LAST * PIECES + q],
+                )
+                for q in range(PIECES)
+            ]
+
+        def go(copies, tracked=True):
+            for copy in copies:
+                copy.start()
+                if tracked:
+                    started.append(copy)
+
+        def arrived(copies):
+            for copy in copies:
+                copy.wait_recv()
 
         prologue(r)
         if r == 0:
             pl.semaphore_wait(barrier, len(near) + len(below) + more)
-        go(cross[0])
-        go(mate[0])
-        go(up[1])
-        go(up[3])
-        go(up[2])
+        for q in range(PIECES):
+            go(cross[0][q : q + 1])
+            go(mate[0][q : q + 1])
+        for j in (1,2,3):
+            go(up[j])
         if r == 0:
             for copy in handoff:
                 copy.start()
@@ -332,22 +353,28 @@
             keep_coefs.start()
             for load in loads[1:]:
                 load.wait()
-        mate[0].wait_recv()
-        up[1].wait_recv()
-        go(mate[1])
-        go(cross[1])
-        cross[0].wait_recv()
-        go(cross[4])
-        mate[1].wait_recv()
-        go(cross[5])
-        for j in (3, 2):
-            up[j].wait_recv()
-            go(mate[j])
-            go(cross[j])
-            mate[j].wait_recv()
-            go(cross[4 + j])
+        behind = []
+
+        def forward(j, q):
+            arrived(mate[j][q : q + 1])
+            go(cross[4 + j][q : q + 1])
+
+        for n, j in enumerate((1,2,3)):
+            for q in range(PIECES):
+                arrived(up[j][q : q + 1])
+                go(mate[j][q : q + 1])
+                go(cross[j][q : q + 1])
+                behind.append((j, q))
+                if len(behind) > BEHIND:
+                    forward(*behind.pop(0))
+            if n == 0:
+                arrived(mate[0])
+                arrived(cross[0])
+                go(cross[4])
+        for j, q in behind:
+            forward(j, q)
         for u in (4, 1, 5):
-            cross[u].wait_recv()
+            arrived(cross[u])
         ffn(r, par, 0, 4 * CAP, psend)
         go(back[5])
         go(back[1])
@@ -358,11 +385,11 @@
         ms[r, 0] = pown[unit(4), :].astype(BF16)
         go(pair[0])
         for u in (2, 6, 3, 7):
-            cross[u].wait_recv()
+            arrived(cross[u])
         ffn(r, par, 4 * CAP, 4 * CAP, psend)
         for u in (7, 3, 6, 2):
             go(back[u])
-        back[4].wait_recv()
+        arrived(back[4])
         psend[r, unit(0), :] = (psend[r, unit(0), :].astype(F32) + ppr[r].astype(F32)).astype(BF16)
         go(back[0])
         if r == 0:
@@ -371,17 +398,20 @@
             coef[0] = split_coefs(routing(pids[...], pwts[...], experts)[1])
 
         def toward_mate(j):
-            back[4 + j].wait_recv()
-            ms[r, j] = (pown[unit(4 + j), :] + rx[r, unit(4 + j), :].astype(F32)).astype(BF16)
-            go(pair[j])
+            for q in range(PIECES):
+                arrived(back[4 + j][q : q + 1])
+                mine, got = pown[unit(4 + j), piece(q)], rx[r, unit(4 + j), piece(q)]
+                ms[r, j, :, piece(q)] = (mine + got.astype(F32)).astype(BF16)
+                go(pair[j][q : q + 1])
 
         def finish(j):
-            back[j].wait_recv()
-            pair[j].wait_recv()
-            fs[r, j] = (
-                pown[unit(j), :] + rx[r, unit(j), :].astype(F32) + rz[r, j].astype(F32)
-            ).astype(BF16)
-            go(last[j], tracked=r == 0 or j > 0)
+            for q in range(PIECES):
+                arrived(back[j][q : q + 1])
+                arrived(pair[j][q : q + 1])
+                mine, got = pown[unit(j), piece(q)], rx[r, unit(j), piece(q)]
+                summed = mine + got.astype(F32) + rz[r, j, :, piece(q)].astype(F32)
+                fs[r, j, :, piece(q)] = summed.astype(BF16)
+                go(last[j][q : q + 1], tracked=r == 0 or j > 0)
 
         toward_mate(1)
         toward_mate(3)
@@ -395,14 +425,15 @@
         finish(0)
         if r == 0:
             for j in (1, 3, 2, 0):
-                last[j].wait_recv()
+                arrived(last[j])
             handoff_arrived()
             epilogue()
             keep_base.start()
         else:
             for j in (1, 3, 2):
-                last[j].wait_recv()
-            last[0].wait()
+                arrived(last[j])
+            for copy in last[0]:
+                copy.wait()
 
     keep_coefs.wait()
     keep_base.wait()
@@ -449,8 +480,8 @@
             pltpu.VMEM((8, tokens), F32),
             pltpu.VMEM((2 * CAP, width), BF16),
             pltpu.VMEM((2, CAP, width), BF16),
-            pltpu.SemaphoreType.DMA((2, CHANNELS)),
-            pltpu.SemaphoreType.DMA((2, CHANNELS)),
+            pltpu.SemaphoreType.DMA((2, CHANNELS * PIECES)),
+            pltpu.SemaphoreType.DMA((2, CHANNELS * PIECES)),
             pltpu.SemaphoreType.DMA((8,)),
             pltpu.SemaphoreType.DMA((8,)),
             pltpu.SemaphoreType.DMA((6,)),

time: 131 us -> 119 us (0.908)
  Pallas kernels: 129 us -> 118 us
    pallas_call x1, Pallas kernels: 126 us -> 115 us  [body(): pl.pallas_call(kernel, out_shape=[jax.ShapeDtypeStruct((tokens, width), B...]
where the time goes in v3:
time: 119 us; the launch traced here: 118 us
  Pallas kernels  118 us (99%)
    pallas_call x1, Pallas kernels, body(): pl.pallas_call(kernel, out_shape=[jax.ShapeDtypeStruct((tokens, width), B...  115 us
    pallas_call x1, Pallas kernels, body(): pl.pallas_call(last_step, out_shape=jax.ShapeDtypeStruct((1, tokens, widt...  2.83 us

profile of v3, /device:TPU:24, one launch (start us, length us, event | category | flops | bytes accessed | tf_op | source)
XLA Modules:
  0.0 118.2 jit_solution(2769754971444899159)
XLA Ops:
  0.0 115.4 %shard_map.73 = (bf16[128,4096]{1,0:T(8,128)(2,1)}, bf16[64,4096]{1,0:T(8,128)(2,1)}, bf16[128,256]{1,0:T(8,128)(2,1)}) custom-call(bf16[128,4096]{1,0:T(8,128)(2,1)} %bitcast.13, bf16[1,4096]{1,0:T(2,128)(2,1)} %gain.1, bf16[4096,384]{1,0:T(8,128)(2,1)} %bitcast.10, bf16[4096,384]{1,0:T(8,128)(2,1)} %bitcast.11, bf16[384,4096]{1,0:T(8,128)(2,1)} %bitcast.12, ...), custom_call_target="tpu_custom_call" | custom-call | flops 4831838208 | bytes 12582912 | tf_op jit(solution)/shard_map/pallas_call | solution.py:451
  115.4 2.8 %shard_map.74 = bf16[1,128,4096]{2,1,0:T(8,128)(2,1)} custom-call(bf16[128,256]{1,0:T(8,128)(2,1)} %get-tuple-element.8.coefs, bf16[64,4096]{1,0:T(8,128)(2,1)} %get-tuple-element.9.results, bf16[128,4096]{1,0:T(8,128)(2,1)} %get-tuple-element.10.carried), custom_call_target="tpu_custom_call" | custom-call | tf_op jit(solution)/shard_map/pallas_call | solution.py:506

commit v4 on v3

--- a/solution.py
+++ b/solution.py
@@ -14,6 +14,7 @@
 UP, MATE, CROSS, BACK, PAIR, LAST = 0, 4, 8, 16, 24, 28
 CHANNELS = 32
 PIECES = 2
+SHARED = 2
 BEHIND = 3
 
 
@@ -298,9 +299,12 @@
         }
         cross = {
             u: channel(own.at[r, unit(u)], par.at[r, unit(u)], CROSS + u, at(0, cross=True))
-            for u in (0, 1, 2, 3, 5, 6, 7)
+            for u in range(8)
+            if u != 4 + SHARED
         }
-        cross[4] = channel(par.at[r, unit(0)], par.at[r, unit(4)], CROSS + 4, at(-dr))
+        cross[4 + SHARED] = channel(
+            par.at[r, unit(SHARED)], par.at[r, unit(4 + SHARED)], CROSS + 4 + SHARED, at(-dr)
+        )
         back = {
             u: channel(psend.at[r, unit(u)], rx.at[r, unit(u)], BACK + u, at(0, cross=True))
             for u in (0, 1, 2, 3, 5, 6, 7)
@@ -342,7 +346,7 @@
         for q in range(PIECES):
             go(cross[0][q : q + 1])
             go(mate[0][q : q + 1])
-        for j in (1,2,3):
+        for j in (1, 2, 3):
             go(up[j])
         if r == 0:
             for copy in handoff:
@@ -357,9 +361,12 @@
 
         def forward(j, q):
             arrived(mate[j][q : q + 1])
-            go(cross[4 + j][q : q + 1])
-
-        for n, j in enumerate((1,2,3)):
+            if j != SHARED:
+                go(cross[4 + j][q : q + 1])
+
+        for q in range(PIECES):
+            forward(0, q)
+        for j in (1, 2, 3):
             for q in range(PIECES):
                 arrived(up[j][q : q + 1])
                 go(mate[j][q : q + 1])
@@ -367,13 +374,12 @@
                 behind.append((j, q))
                 if len(behind) > BEHIND:
                     forward(*behind.pop(0))
-            if n == 0:
-                arrived(mate[0])
-                arrived(cross[0])
-                go(cross[4])
+        for q in range(PIECES):
+            arrived(cross[SHARED][q : q + 1])
+            go(cross[4 + SHARED][q : q + 1])
         for j, q in behind:
             forward(j, q)
-        for u in (4, 1, 5):
+        for u in (0, 4, 1, 5):
             arrived(cross[u])
         ffn(r, par, 0, 4 * CAP, psend)
         go(back[5])
@@ -384,7 +390,7 @@
         ffn(r, own, 0, 8 * CAP, pown)
         ms[r, 0] = pown[unit(4), :].astype(BF16)
         go(pair[0])
-        for u in (2, 6, 3, 7):
+        for u in (6, 3, 7):
             arrived(cross[u])
         ffn(r, par, 4 * CAP, 4 * CAP, psend)
         for u in (7, 3, 6, 2):
@@ -430,16 +436,18 @@
             epilogue()
             keep_base.start()
         else:
+            for copy in started[: -2 * PIECES] + handoff:
+                copy.wait_send()
+            handoff_sent()
+            keep_coefs.wait()
+            keep_base.wait()
             for j in (1, 3, 2):
                 arrived(last[j])
             for copy in last[0]:
                 copy.wait()
 
-    keep_coefs.wait()
-    keep_base.wait()
-    for copy in started + handoff:
+    for copy in started[-2 * PIECES :]:
         copy.wait_send()
-    handoff_sent()
 
 
 def body(activations, norm_gain, w_gate, w_up, w_down, expert_ids, route_weights):

time: 119 us -> 116 us (0.975)
  Pallas kernels: 118 us -> 116 us
    pallas_call x1, Pallas kernels: 115 us -> 113 us  [body(): pl.pallas_call(kernel, out_shape=[jax.ShapeDtypeStruct((tokens, width), B...]
where the time goes in v4:
time: 116 us
  Pallas kernels  116 us (100%)
    pallas_call x1, Pallas kernels, body(): pl.pallas_call(kernel, out_shape=[jax.ShapeDtypeStruct((tokens, width), B...  113 us
    pallas_call x1, Pallas kernels, body(): pl.pallas_call(last_step, out_shape=jax.ShapeDtypeStruct((1, tokens, widt...  2.83 us

profile of v4, /device:TPU:24, one launch (start us, length us, event | category | flops | bytes accessed | tf_op | source)
XLA Modules:
  0.0 116.3 jit_solution(3041460679328188086)
XLA Ops:
  0.0 113.5 %shard_map.73 = (bf16[128,4096]{1,0:T(8,128)(2,1)}, bf16[64,4096]{1,0:T(8,128)(2,1)}, bf16[128,256]{1,0:T(8,128)(2,1)}) custom-call(bf16[128,4096]{1,0:T(8,128)(2,1)} %bitcast.13, bf16[1,4096]{1,0:T(2,128)(2,1)} %gain.1, bf16[4096,384]{1,0:T(8,128)(2,1)} %bitcast.10, bf16[4096,384]{1,0:T(8,128)(2,1)} %bitcast.11, bf16[384,4096]{1,0:T(8,128)(2,1)} %bitcast.12, ...), custom_call_target="tpu_custom_call" | custom-call | flops 4831838208 | bytes 12582912 | tf_op jit(solution)/shard_map/pallas_call | solution.py:459
  113.5 2.8 %shard_map.74 = bf16[1,128,4096]{2,1,0:T(8,128)(2,1)} custom-call(bf16[128,256]{1,0:T(8,128)(2,1)} %get-tuple-element.8.coefs, bf16[64,4096]{1,0:T(8,128)(2,1)} %get-tuple-element.9.results, bf16[128,4096]{1,0:T(8,128)(2,1)} %get-tuple-element.10.carried), custom_call_target="tpu_custom_call" | custom-call | tf_op jit(solution)/shard_map/pallas_call | solution.py:514

commit v5 on v4

--- a/solution.py
+++ b/solution.py
@@ -351,7 +351,6 @@
         if r == 0:
             for copy in handoff:
                 copy.start()
-            handoff_start()
             sel[1], coefs = routing(ids[1], weights[1], experts)
             coef[1] = split_coefs(coefs)
             keep_coefs.start()
@@ -379,14 +378,14 @@
             go(cross[4 + SHARED][q : q + 1])
         for j, q in behind:
             forward(j, q)
+        if r == 0:
+            handoff_start()
         for u in (0, 4, 1, 5):
             arrived(cross[u])
         ffn(r, par, 0, 4 * CAP, psend)
         go(back[5])
         go(back[1])
         go(back[4])
-        if r == 0:
-            handoff_over()
         ffn(r, own, 0, 8 * CAP, pown)
         ms[r, 0] = pown[unit(4), :].astype(BF16)
         go(pair[0])
@@ -402,6 +401,7 @@
             handoff[0].wait_recv()
             handoff[1].wait_recv()
             coef[0] = split_coefs(routing(pids[...], pwts[...], experts)[1])
+            handoff_over()
 
         def toward_mate(j):
             for q in range(PIECES):

time: 116 us -> 115 us (level)
  the two profiles are of different devices: /device:TPU:24 before, /device:TPU:34 now
where the time goes in v5:
time: 115 us
  Pallas kernels  115 us (100%)
    pallas_call x1, Pallas kernels, body(): pl.pallas_call(kernel, out_shape=[jax.ShapeDtypeStruct((tokens, width), B...  112 us
    pallas_call x1, Pallas kernels, body(): pl.pallas_call(last_step, out_shape=jax.ShapeDtypeStruct((1, tokens, widt...  2.83 us

profile of v5, /device:TPU:34, one launch (start us, length us, event | category | flops | bytes accessed | tf_op | source)
XLA Modules:
  0.0 115.1 jit_solution(4388947020326589565)
XLA Ops:
  0.0 112.3 %shard_map.73 = (bf16[128,4096]{1,0:T(8,128)(2,1)}, bf16[64,4096]{1,0:T(8,128)(2,1)}, bf16[128,256]{1,0:T(8,128)(2,1)}) custom-call(bf16[128,4096]{1,0:T(8,128)(2,1)} %bitcast.13, bf16[1,4096]{1,0:T(2,128)(2,1)} %gain.1, bf16[4096,384]{1,0:T(8,128)(2,1)} %bitcast.10, bf16[4096,384]{1,0:T(8,128)(2,1)} %bitcast.11, bf16[384,4096]{1,0:T(8,128)(2,1)} %bitcast.12, ...), custom_call_target="tpu_custom_call" | custom-call | flops 4831838208 | bytes 12582912 | tf_op jit(solution)/shard_map/pallas_call | solution.py:459
  112.3 2.8 %shard_map.74 = bf16[1,128,4096]{2,1,0:T(8,128)(2,1)} custom-call(bf16[128,256]{1,0:T(8,128)(2,1)} %get-tuple-element.8.coefs, bf16[64,4096]{1,0:T(8,128)(2,1)} %get-tuple-element.9.results, bf16[128,4096]{1,0:T(8,128)(2,1)} %get-tuple-element.10.carried), custom_call_target="tpu_custom_call" | custom-call | tf_op jit(solution)/shard_map/pallas_call | solution.py:514
